TPU v7x, 32 devices: a whole 2x2x4 slice. The times are simulated.
32 devices in a mesh: tile: 16 (over z, y, x), exp: 2 (over core).
Axes of the slice: x: 2, y: 2, z: 4, core: 2. Of those that a mesh axis runs over, the one named last changes fastest.
Arguments:
- initial: float32 [3, 1024, 256], P(None, ('exp', 'tile')), parts along dimension 1, may hold values from -6 to 6
- depth_field: float32 [1024, 256], P(('exp', 'tile')), parts along dimension 0, may hold values from 0.5 to 2
- coriolis: float32 [1024, 256], P(('exp', 'tile')), parts along dimension 0, may hold values from -1 to 1
- cell_area: float32 [1024, 256], P(('exp', 'tile')), parts along dimension 0, may hold values from 1 to 2
- face_len: float32 [2, 1024, 256], P(None, ('exp', 'tile')), parts along dimension 1, may hold values from 0.5 to 1
- owners: int32 [2048, 2], P(('exp', 'tile')), parts along dimension 0, may hold values from 0 to 15, as said below
- offsets: int32 [2048, 2], P(('exp', 'tile')), parts along dimension 0, may hold values from 0 to 15
- weights: bfloat16 [2048, 2, 128, 128], P(('exp', 'tile')), parts along dimension 0, may hold values from -0.25 to 0.25
Outputs:
- remapped: float32 [512, 4, 128], P(('exp', 'tile')), parts along dimension 0
- final_fields: float32 [3, 1024, 256], P(None, ('exp', 'tile')), parts along dimension 1
There are 2 independent parts, one for each index of `exp`. A program takes and returns all parts, laid end to end along the dimension named above; each array names one. Nothing has to cross between parts.
Inputs may be any that keep to these rules, and one draw needn't show every extreme that they name: `owners`: of the 128 intersections of one device's source blocks, at most 16 name the same owner; in every draw one owner is named by exactly 16 intersections of every device.
All inputs are finite; a program needn't handle non-finite values.
Results may differ from a plain program's by a relative error of at most 0.0029.
Values sent between devices are 32-bit elements; how exact they have to be, the bound alone decides.
A program may use at most 64 MiB of HBM per device.

v0:
```python
import jax
import jax.numpy as jnp
from jax import lax
from jax.sharding import PartitionSpec as P

STEPS = 4
TB = 16


time_step = 0.3


def with_halo(cells, sides, width):
    for axis, dim in sides:
        count = lax.axis_size(axis)
        head = lax.slice_in_dim(cells, 0, width, axis=dim)
        tail = lax.slice_in_dim(cells, cells.shape[dim] - width, cells.shape[dim], axis=dim)
        cells = jnp.concatenate(
            [
                lax.ppermute(tail, axis, [(i, (i + 1) % count) for i in range(count)]),
                cells,
                lax.ppermute(head, axis, [((i + 1) % count, i) for i in range(count)]),
            ],
            axis=dim,
        )
    return cells


def advance(fields, metric):
    height, speed_x, speed_y = (fields[0], fields[1], fields[2])
    depth, rotation, area, east_len, north_len = (
        metric[0],
        metric[1],
        metric[2],
        metric[3],
        metric[4],
    )
    wave_x = jnp.sqrt(jnp.maximum(depth[:-1], depth[1:]))
    edge = east_len[:-1]
    flux_h = edge * (
        0.5 * (depth[:-1] * speed_x[:-1] + depth[1:] * speed_x[1:])
        - 0.5 * wave_x * (height[1:] - height[:-1])
    )
    flux_u = edge * (0.5 * (height[:-1] + height[1:]) - 0.5 * wave_x * (speed_x[1:] - speed_x[:-1]))
    flux_v = edge * (-0.5 * wave_x * (speed_y[1:] - speed_y[:-1]))
    own_h = height[1:-1]
    own_u = speed_x[1:-1]
    own_v = speed_y[1:-1]
    own_d = depth[1:-1]
    own_f = rotation[1:-1]
    own_a = area[1:-1]
    own_n = north_len[1:-1]
    above_h = jnp.concatenate([own_h[:, 1:], own_h[:, -1:]], axis=1)
    above_u = jnp.concatenate([own_u[:, 1:], own_u[:, -1:]], axis=1)
    above_v = jnp.concatenate([own_v[:, 1:], -own_v[:, -1:]], axis=1)
    above_d = jnp.concatenate([own_d[:, 1:], own_d[:, -1:]], axis=1)
    wave_y = jnp.sqrt(jnp.maximum(own_d, above_d))
    north_h = own_n * (0.5 * (own_d * own_v + above_d * above_v) - 0.5 * wave_y * (above_h - own_h))
    north_u = own_n * (-0.5 * wave_y * (above_u - own_u))
    north_v = own_n * (0.5 * (own_h + above_h) - 0.5 * wave_y * (above_v - own_v))
    wall_v = own_n[:, :1] * (own_h[:, :1] - jnp.sqrt(own_d[:, :1]) * own_v[:, :1])
    zeros = jnp.zeros_like(wall_v)
    south_h = jnp.concatenate([zeros, north_h[:, :-1]], axis=1)
    south_u = jnp.concatenate([zeros, north_u[:, :-1]], axis=1)
    south_v = jnp.concatenate([wall_v, north_v[:, :-1]], axis=1)
    factor = time_step / own_a
    new_h = own_h - factor * (flux_h[1:] - flux_h[:-1] + north_h - south_h)
    new_u = (
        own_u - factor * (flux_u[1:] - flux_u[:-1] + north_u - south_u) + time_step * own_f * own_v
    )
    new_v = (
        own_v - factor * (flux_v[1:] - flux_v[:-1] + north_v - south_v) - time_step * own_f * own_u
    )
    return jnp.stack([new_h, new_u, new_v])


def on_device(initial, depth_field, coriolis, cell_area, face_len, owners, offsets, weights):
    metric = jnp.concatenate([jnp.stack([depth_field, coriolis, cell_area]), face_len], axis=0)
    snapshots = []
    metric_ext = with_halo(metric, (("tile", 1),), 1)
    fields = initial
    for number in range(STEPS):
        fields = advance(with_halo(fields, (("tile", 1),), 1), metric_ext)
        snapshots.append(fields[0])
    snapped = jnp.stack(snapshots).astype(jnp.bfloat16).reshape(STEPS, -1, 128)
    contribution = jnp.einsum(
        "sbk,brkt->brst", snapped, weights, preferred_element_type=jnp.float32
    )
    slot_count = weights.shape[0] * weights.shape[1]
    flat = contribution.reshape(slot_count, STEPS * 128)
    owner_list = owners.reshape(-1)
    offset_list = offsets.reshape(-1)
    target = owner_list * TB + offset_list
    rows_here = jnp.arange(TB * lax.axis_size("tile"), dtype=jnp.int32)
    select = (rows_here[:, None] == target[None, :]).astype(jnp.float32)
    gathered = lax.psum_scatter(
        jnp.dot(select, flat, precision=lax.Precision.HIGHEST, preferred_element_type=jnp.float32),
        "tile",
        scatter_dimension=0,
        tiled=True,
    )
    return (gathered.reshape(TB, STEPS, 128), fields)


def solution(mesh):
    placed = (
        P(None, ("exp", "tile"), None),
        P(("exp", "tile"), None),
        P(("exp", "tile"), None),
        P(("exp", "tile"), None),
        P(None, ("exp", "tile"), None),
        P(("exp", "tile"), None),
        P(("exp", "tile"), None),
        P(("exp", "tile"), None, None, None),
    )
    return jax.shard_map(
        on_device,
        mesh=mesh,
        in_specs=placed,
        out_specs=(P(("exp", "tile"), None, None), P(None, ("exp", "tile"), None)),
        check_vma=False,
    )
```

profile of v0, /device:TPU:0, one launch (start us, length us, event | category | flops | bytes accessed | tf_op | source)
XLA Modules:
  0.0 143.4 jit_solution(1618315999390051213)
XLA Ops:
  7.3 0.8 pad_maximum_fusion.23
  8.1 3.0 %collective-permute-start = (f32[5,1,256]{2,1,0:T(1,128)S(1)}, f32[5,1,256]{2,1,0:T(1,128)S(1)}, u32[]{:S(2)}, u32[]{:S(2)}) collective-permute-start(f32[5,1,256]{2,1,0:T(1,128)S(1)} %get-tuple-element.39), channel_id=1, source_target_pairs={{0,2},{2,4},{4,6},{6,8},{8,10},{10,12},{12,14},{14,16},{16,18},{18... | collective-permute-start | bytes 15368 | tf_op jit(solution)/shard_map/ppermute | solution.py:20
  11.1 4.1 %collective-permute-start.2 = (f32[5,1,256]{2,1,0:T(1,128)S(1)}, f32[5,1,256]{2,1,0:T(1,128)S(1)}, u32[]{:S(2)}, u32[]{:S(2)}) collective-permute-start(f32[5,1,256]{2,1,0:T(1,128)S(1)} %get-tuple-element.38), channel_id=1, source_target_pairs={{2,0},{4,2},{6,4},{8,6},{10,8},{12,10},{14,12},{16,14},{18,16},{20... | collective-permute-start | bytes 15368 | tf_op jit(solution)/shard_map/ppermute | solution.py:22
  15.9 2.0 %collective-permute-start.3 = (f32[3,1,256]{2,1,0:T(1,128)S(1)}, f32[3,1,256]{2,1,0:T(1,128)S(1)}, u32[]{:S(2)}, u32[]{:S(2)}) collective-permute-start(f32[3,1,256]{2,1,0:T(1,128)S(1)} %get-tuple-element.59), channel_id=1, source_target_pairs={{2,0},{4,2},{6,4},{8,6},{10,8},{12,10},{14,12},{16,14},{18,16},{20... | collective-permute-start | bytes 9224 | tf_op jit(solution)/shard_map/ppermute | solution.py:22
  19.5 0.8 slice.600
  20.6 0.8 fusion.107
  22.1 0.9 fusion.93
  23.0 0.9 subtract_multiply_fusion.14
  23.9 0.9 constant_dynamic-update-slice_fusion
  25.2 0.9 subtract_multiply_fusion.6
  26.1 0.8 fusion.21
  26.9 0.9 fusion.109
  27.9 0.9 fusion.86
  28.8 0.8 fusion.105
  29.9 5.6 %collective-permute-start.5 = (f32[3,1,256]{2,1,0:T(1,128)S(1)}, f32[3,1,256]{2,1,0:T(1,128)S(1)}, u32[]{:S(2)}, u32[]{:S(2)}) collective-permute-start(f32[3,1,256]{2,1,0:T(1,128)S(1)} %get-tuple-element.56), channel_id=1, source_target_pairs={{2,0},{4,2},{6,4},{8,6},{10,8},{12,10},{14,12},{16,14},{18,16},{20... | collective-permute-start | bytes 9224 | tf_op jit(solution)/shard_map/ppermute | solution.py:22
  35.5 0.9 subtract_multiply_fusion.12
  37.7 5.7 %collective-permute-start.7 = (f32[3,1,256]{2,1,0:T(1,128)S(1)}, f32[3,1,256]{2,1,0:T(1,128)S(1)}, u32[]{:S(2)}, u32[]{:S(2)}) collective-permute-start(f32[3,1,256]{2,1,0:T(1,128)S(1)} %get-tuple-element.52), channel_id=1, source_target_pairs={{2,0},{4,2},{6,4},{8,6},{10,8},{12,10},{14,12},{16,14},{18,16},{20... | collective-permute-start | bytes 9224 | tf_op jit(solution)/shard_map/ppermute | solution.py:22
  43.5 1.3 collective-permute-done.6
  45.5 5.7 %collective-permute-start.9 = (f32[3,1,256]{2,1,0:T(1,128)S(1)}, f32[3,1,256]{2,1,0:T(1,128)S(1)}, u32[]{:S(2)}, u32[]{:S(2)}) collective-permute-start(f32[3,1,256]{2,1,0:T(1,128)S(1)} %get-tuple-element.48), channel_id=1, source_target_pairs={{2,0},{4,2},{6,4},{8,6},{10,8},{12,10},{14,12},{16,14},{18,16},{20... | collective-permute-start | bytes 9224 | tf_op jit(solution)/shard_map/ppermute | solution.py:22
  51.4 1.3 collective-permute-done.8
  52.9 2.9 %fusion.3 = f32[64,4,2,128]{3,1,2,0:T(4,128)S(1)} fusion(bf16[64,2,128,128]{3,2,1,0:T(8,128)(2,1)} %param.15, bf16[1,64,128]{2,0,1:T(2,128)(2,1)S(1)} %stack.95, bf16[1,64,128]{2,0,1:T(2,128)(2,1)S(1)} %stack.94, bf16[1,64,128]{2,0,1:T(2,128)(2,1)S(1)} %stack.93, bf16[1,64,128]{2,0,1:T(2,128)(2,1)S(1)} %stack.92), kind=kOutput, calls=%fused_computation.16 | convolution fusion | flops 17039360 | bytes 4521984 | tf_op jit(solution)/shard_map/sbk,brkt->brst/dot_general | solution.py:86
  55.8 1.2 fusion
  57.6 77.5 %reduce-scatter.2.cloned.1.call-done = f32[16,512]{1,0:T(8,128)} async-done(((f32[256,512]{1,0:T(8,128)}), f32[16,512]{1,0:T(8,128)}) %reduce-scatter.2.cloned.1.call-update) | async-done | bytes 32784 | tf_op jit(solution)/shard_map/reduce_scatter | solution.py:96
  135.2 1.4 reshape.156
  (69 shorter events, 7.2 us)
Async XLA Ops:
  7.2 30.1 %copy-start = (f32[32,256]{1,0:T(8,128)S(1)}, f32[32,256]{1,0:T(8,128)}, u32[]{:S(2)}) copy-start(f32[32,256]{1,0:T(8,128)} %param.9) | copy-start | bytes 98308
  7.2 29.9 %copy-start.3 = (f32[32,256]{1,0:T(8,128)S(1)}, f32[32,256]{1,0:T(8,128)}, u32[]{:S(2)}) copy-start(f32[32,256]{1,0:T(8,128)} %param.10) | copy-start | bytes 98308
  7.2 29.9 %copy-start.2 = (f32[32,256]{1,0:T(8,128)S(1)}, f32[32,256]{1,0:T(8,128)}, u32[]{:S(2)}) copy-start(f32[32,256]{1,0:T(8,128)} %param.11) | copy-start | bytes 98308
  7.2 29.1 %copy-start.1 = (f32[2,32,256]{2,1,0:T(8,128)S(1)}, f32[2,32,256]{2,1,0:T(8,128)}, u32[]{:S(2)}) copy-start(f32[2,32,256]{2,1,0:T(8,128)} %param.12) | copy-start | bytes 196612
  7.2 128.0 %reduce-scatter.2.cloned.1.call-start = ((), (), s32[]{:S(2)}) async-start(), calls=%async_computation.1 | async-start | bytes 557056 | tf_op jit(solution)/shard_map/reduce_scatter | solution.py:96
  8.1 17.1 %collective-permute-start = (f32[5,1,256]{2,1,0:T(1,128)S(1)}, f32[5,1,256]{2,1,0:T(1,128)S(1)}, u32[]{:S(2)}, u32[]{:S(2)}) collective-permute-start(f32[5,1,256]{2,1,0:T(1,128)S(1)} %get-tuple-element.39), channel_id=1, source_target_pairs={{0,2},{2,4},{4,6},{6,8},{8,10},{10,12},{12,14},{14,16},{16,18},{18... | collective-permute-start | bytes 15368 | tf_op jit(solution)/shard_map/ppermute | solution.py:20
  11.1 14.1 %collective-permute-start.2 = (f32[5,1,256]{2,1,0:T(1,128)S(1)}, f32[5,1,256]{2,1,0:T(1,128)S(1)}, u32[]{:S(2)}, u32[]{:S(2)}) collective-permute-start(f32[5,1,256]{2,1,0:T(1,128)S(1)} %get-tuple-element.38), channel_id=1, source_target_pairs={{2,0},{4,2},{6,4},{8,6},{10,8},{12,10},{14,12},{16,14},{18,16},{20... | collective-permute-start | bytes 15368 | tf_op jit(solution)/shard_map/ppermute | solution.py:22
  15.9 9.2 %collective-permute-start.3 = (f32[3,1,256]{2,1,0:T(1,128)S(1)}, f32[3,1,256]{2,1,0:T(1,128)S(1)}, u32[]{:S(2)}, u32[]{:S(2)}) collective-permute-start(f32[3,1,256]{2,1,0:T(1,128)S(1)} %get-tuple-element.59), channel_id=1, source_target_pairs={{2,0},{4,2},{6,4},{8,6},{10,8},{12,10},{14,12},{16,14},{18,16},{20... | collective-permute-start | bytes 9224 | tf_op jit(solution)/shard_map/ppermute | solution.py:22
  17.9 7.3 %collective-permute-start.1 = (f32[3,1,256]{2,1,0:T(1,128)S(1)}, f32[3,1,256]{2,1,0:T(1,128)S(1)}, u32[]{:S(2)}, u32[]{:S(2)}) collective-permute-start(f32[3,1,256]{2,1,0:T(1,128)S(1)} %get-tuple-element.58), channel_id=1, source_target_pairs={{0,2},{2,4},{4,6},{6,8},{8,10},{10,12},{12,14},{14,16},{16,18},{18... | collective-permute-start | bytes 9224 | tf_op jit(solution)/shard_map/ppermute | solution.py:20
  29.8 7.2 %collective-permute-start.4 = (f32[3,1,256]{2,1,0:T(1,128)S(1)}, f32[3,1,256]{2,1,0:T(1,128)S(1)}, u32[]{:S(2)}, u32[]{:S(2)}) collective-permute-start(f32[3,1,256]{2,1,0:T(1,128)S(1)} %get-tuple-element.57), channel_id=1, source_target_pairs={{0,2},{2,4},{4,6},{6,8},{8,10},{10,12},{12,14},{14,16},{16,18},{18... | collective-permute-start | bytes 9224 | tf_op jit(solution)/shard_map/ppermute | solution.py:20
  29.9 7.2 %collective-permute-start.5 = (f32[3,1,256]{2,1,0:T(1,128)S(1)}, f32[3,1,256]{2,1,0:T(1,128)S(1)}, u32[]{:S(2)}, u32[]{:S(2)}) collective-permute-start(f32[3,1,256]{2,1,0:T(1,128)S(1)} %get-tuple-element.56), channel_id=1, source_target_pairs={{2,0},{4,2},{6,4},{8,6},{10,8},{12,10},{14,12},{16,14},{18,16},{20... | collective-permute-start | bytes 9224 | tf_op jit(solution)/shard_map/ppermute | solution.py:22
  37.6 7.2 %collective-permute-start.6 = (f32[3,1,256]{2,1,0:T(1,128)S(1)}, f32[3,1,256]{2,1,0:T(1,128)S(1)}, u32[]{:S(2)}, u32[]{:S(2)}) collective-permute-start(f32[3,1,256]{2,1,0:T(1,128)S(1)} %get-tuple-element.53), channel_id=1, source_target_pairs={{0,2},{2,4},{4,6},{6,8},{8,10},{10,12},{12,14},{14,16},{16,18},{18... | collective-permute-start | bytes 9224 | tf_op jit(solution)/shard_map/ppermute | solution.py:20
  37.7 7.2 %collective-permute-start.7 = (f32[3,1,256]{2,1,0:T(1,128)S(1)}, f32[3,1,256]{2,1,0:T(1,128)S(1)}, u32[]{:S(2)}, u32[]{:S(2)}) collective-permute-start(f32[3,1,256]{2,1,0:T(1,128)S(1)} %get-tuple-element.52), channel_id=1, source_target_pairs={{2,0},{4,2},{6,4},{8,6},{10,8},{12,10},{14,12},{16,14},{18,16},{20... | collective-permute-start | bytes 9224 | tf_op jit(solution)/shard_map/ppermute | solution.py:22
  45.4 7.3 %collective-permute-start.8 = (f32[3,1,256]{2,1,0:T(1,128)S(1)}, f32[3,1,256]{2,1,0:T(1,128)S(1)}, u32[]{:S(2)}, u32[]{:S(2)}) collective-permute-start(f32[3,1,256]{2,1,0:T(1,128)S(1)} %get-tuple-element.49), channel_id=1, source_target_pairs={{0,2},{2,4},{4,6},{6,8},{8,10},{10,12},{12,14},{14,16},{16,18},{18... | collective-permute-start | bytes 9224 | tf_op jit(solution)/shard_map/ppermute | solution.py:20
  45.5 7.2 %collective-permute-start.9 = (f32[3,1,256]{2,1,0:T(1,128)S(1)}, f32[3,1,256]{2,1,0:T(1,128)S(1)}, u32[]{:S(2)}, u32[]{:S(2)}) collective-permute-start(f32[3,1,256]{2,1,0:T(1,128)S(1)} %get-tuple-element.48), channel_id=1, source_target_pairs={{2,0},{4,2},{6,4},{8,6},{10,8},{12,10},{14,12},{16,14},{18,16},{20... | collective-permute-start | bytes 9224 | tf_op jit(solution)/shard_map/ppermute | solution.py:22
Sparse Core Ops, SparseCore 0:
  57.1 77.9 reduce-scatter.1
where the time goes:
time: 145 us; the launch traced here: 143 us
  waiting for transfers between devices  80.8 us (56%)
  starting transfers between devices  26.3 us (18%)
  between operations  14.2 us (10%)
  other arithmetic  11.1 us (8%)
  local copies, waits for them, and re-layouts  6.98 us (5%)
  matrix products  4.04 us (3%)
    reduce_scatter x1, waiting for transfers between devices, on_device(): lax.psum_scatter(jnp.dot(select, flat, precision=lax.Precision.HIGHEST, p...  77.5 us
    ppermute x5, starting transfers between devices, with_halo(): lax.ppermute(head, axis, [((i + 1) % count, i) for i in range(count)])  23 us
    ppermute x5, waiting for transfers between devices, with_halo(): lax.ppermute(tail, axis, [(i, (i + 1) % count) for i in range(count)])  3.25 us
    ppermute x5, starting transfers between devices, with_halo(): lax.ppermute(tail, axis, [(i, (i + 1) % count) for i in range(count)])  3.21 us
  transfers between devices with their start and end apart: 11, of which 4 were waited for; matrix products, arithmetic and copies ran while one was open for 7% of the time, Pallas kernels for 0%

commit v1 on v0

v1 whole, which is shorter than its diff:
```python
import functools

import jax
import jax.numpy as jnp
from jax import lax
from jax.experimental import pallas as pl
from jax.experimental.pallas import tpu as pltpu
from jax.sharding import PartitionSpec as P

STEPS = 4
TB = 16
TIME_STEP = 0.3
INNER = 4
HALO = 4
CHUNKS = ((0, 1), (2, 3))
WEIGHT_PARTS = 4
MESH = pl.DeviceIdType.MESH


def kernel(
    n,
    init_ref,
    depth_ref,
    cor_ref,
    area_ref,
    face_ref,
    own_ref,
    off_ref,
    w_ref,
    out_ref,
    fin_ref,
    st,
    wv,
    hs,
    hr,
    sd,
    cc,
    sel,
    s1,
    r1,
    s2,
    r2,
    load_sem,
    w_sem,
    hs_sem,
    hr_sem,
    s1_sem,
    r1_sem,
    s2_sem,
    r2_sem,
    fin_sem,
):
    cols = init_ref.shape[1]
    ny = init_ref.shape[2]
    ext = cols + 2 * HALO
    blocks = w_ref.shape[0]
    reps = w_ref.shape[1]
    groups = n // INNER
    rows = n * TB
    me = lax.axis_index("tile")
    mine = lax.rem(me, INNER)
    group = me // INNER
    left = lax.rem(me + n - 1, n)
    right = lax.rem(me + 1, n)
    mates = [group * INNER + lax.rem(mine + d, INNER) for d in range(1, INNER)]
    peers = [lax.rem(group + d, groups) * INNER + mine for d in range(1, groups)]

    own_rows = pl.ds(0, cols)
    loads = [
        pltpu.make_async_copy(init_ref, st.at[pl.ds(0, 3), own_rows], load_sem.at[0]),
        pltpu.make_async_copy(depth_ref, st.at[3, own_rows], load_sem.at[1]),
        pltpu.make_async_copy(cor_ref, st.at[4, own_rows], load_sem.at[2]),
        pltpu.make_async_copy(area_ref, st.at[5, own_rows], load_sem.at[3]),
        pltpu.make_async_copy(face_ref, st.at[pl.ds(6, 2), own_rows], load_sem.at[4]),
    ]
    for copy in loads:
        copy.start()
    part = blocks // WEIGHT_PARTS
    w_loads = [
        pltpu.make_async_copy(
            w_ref.at[pl.ds(i * part, part)], wv.at[pl.ds(i * part, part)], w_sem.at[i]
        )
        for i in range(WEIGHT_PARTS)
    ]
    barrier = pltpu.get_barrier_semaphore()
    partners = [left, right] + mates + peers
    for partner in partners:
        pl.semaphore_signal(barrier, inc=1, device_id={"tile": partner}, device_id_type=MESH)
    for copy in w_loads:
        copy.start()
    for copy in loads:
        copy.wait()

    low = lax.broadcasted_iota(jnp.int32, (8, ny), 0) < HALO
    for a in range(4):
        even, odd = st[2 * a, 0:8, :], st[2 * a + 1, 0:8, :]
        hs[0, a] = jnp.where(low, even, pltpu.roll(odd, HALO, 0))
        even, odd = st[2 * a, cols - 8 : cols, :], st[2 * a + 1, cols - 8 : cols, :]
        hs[1, a] = jnp.where(low, pltpu.roll(odd, HALO, 0), even)
    pl.semaphore_wait(barrier, len(partners))
    halos = [
        pltpu.make_async_remote_copy(
            src_ref=hs.at[i],
            dst_ref=hr.at[i],
            send_sem=hs_sem.at[i],
            recv_sem=hr_sem.at[i],
            device_id={"tile": to},
            device_id_type=MESH,
        )
        for i, to in enumerate((left, right))
    ]
    for copy in halos:
        copy.start()

    sd[...] = jnp.zeros_like(sd)
    owner = own_ref[...]
    target = (owner % INNER) * (groups * TB) + (owner // INNER) * TB + off_ref[...]
    place = lax.broadcasted_iota(jnp.int32, (blocks, rows), 1)
    hot = jnp.concatenate(
        [jnp.where(place == target[:, r : r + 1], 1.0, 0.0) for r in range(reps)], axis=0
    )
    hot = hot.T.astype(jnp.bfloat16)
    sel[...] = jnp.concatenate([hot, hot], axis=1)

    for copy in halos:
        copy.wait()
    for a in range(4):
        after, before = hr[0, a], hr[1, a]
        st[2 * a, cols:ext, :] = jnp.where(low, after, before)
        st[2 * a + 1, cols:ext, :] = jnp.where(
            low, pltpu.roll(after, HALO, 0), pltpu.roll(before, HALO, 0)
        )

    def east(x):
        return pltpu.roll(x, ext - 1, 0)

    def west(x):
        return pltpu.roll(x, 1, 0)

    def north(x):
        return pltpu.roll(x, ny - 1, 1)

    def south(x):
        return pltpu.roll(x, 1, 1)

    lane = lax.broadcasted_iota(jnp.int32, (ext, ny), 1)
    first, last = lane == 0, lane == ny - 1
    depth = st[3]
    turn = TIME_STEP * st[4]
    factor = TIME_STEP / st[5]
    half_x = 0.5 * st[6]
    wave_x = half_x * jnp.sqrt(jnp.maximum(depth, east(depth)))
    n_len = st[7]
    half_y = jnp.where(last, 0.0, 0.5 * n_len)
    wave_y = half_y * jnp.sqrt(jnp.maximum(depth, north(depth)))
    wall_h = jnp.where(first, -n_len, jnp.where(last, n_len, 0.0))
    wall_v = jnp.where(first | last, n_len * jnp.sqrt(depth), 0.0)

    def advance(h, u, v):
        q = depth * u
        he, ue, ve = east(h), east(u), east(v)
        fh = half_x * (q + east(q)) - wave_x * (he - h)
        fu = half_x * (h + he) - wave_x * (ue - u)
        fv = wave_x * (v - ve)
        p = depth * v
        hn, un, vn = north(h), north(u), north(v)
        gh = half_y * (p + north(p)) - wave_y * (hn - h)
        gu = wave_y * (u - un)
        gv = half_y * (h + hn) - wave_y * (vn - v)
        new_h = h - factor * (fh - west(fh) + gh - south(gh))
        new_u = u - factor * (fu - west(fu) + gu - south(gu)) + turn * v
        new_v = (
            v - factor * (fv - west(fv) + gv - south(gv) + wall_h * h + wall_v * v) - turn * u
        )
        return new_h, new_u, new_v

    fin_copy = pltpu.make_async_copy(st.at[pl.ds(0, 3), own_rows], fin_ref, fin_sem)

    def remote(src, dst, send, recv, to):
        return pltpu.make_async_remote_copy(
            src_ref=src,
            dst_ref=dst,
            send_sem=send,
            recv_sem=recv,
            device_id={"tile": to},
            device_id_type=MESH,
        )

    inner_copies = [
        [
            remote(
                s1.at[lax.rem(mine + d, INNER), k],
                r1.at[d - 1, k],
                s1_sem.at[d - 1, k],
                r1_sem.at[d - 1, k],
                mates[d - 1],
            )
            for d in range(1, INNER)
        ]
        for k in range(len(CHUNKS))
    ]
    outer_copies = [
        [
            remote(
                s2.at[lax.rem(group + d, groups), k],
                r2.at[d - 1, k],
                s2_sem.at[d - 1, k],
                r2_sem.at[d - 1, k],
                peers[d - 1],
            )
            for d in range(1, groups)
        ]
        for k in range(len(CHUNKS))
    ]

    def second_phase(k):
        for copy in inner_copies[k]:
            copy.wait_recv()
        total = s1[mine, k]
        for d in range(1, INNER):
            total = total + r1[d - 1, k]
        for g in range(groups):
            s2[g, k] = total[:, g * TB : (g + 1) * TB, :]
        for copy in outer_copies[k]:
            copy.start()

    h, u, v = st[0], st[1], st[2]
    for k, chunk in enumerate(CHUNKS):
        for step in chunk:
            h, u, v = advance(h, u, v)
            sd[0, pl.ds(step, cols, stride=8), :] = h[:cols, :128]
            sd[1, pl.ds(STEPS + step, cols, stride=8), :] = h[:cols, 128:]
        if k == len(CHUNKS) - 1:
            st[0], st[1], st[2] = h, u, v
            fin_copy.start()
        if k == 0:
            for copy in w_loads:
                copy.wait()

        def product(c, carry):
            at = pl.ds(pl.multiple_of(c * 8, 8), 8)
            lhs = jnp.concatenate([sd[0, at, :], sd[1, at, :]], axis=1).astype(jnp.bfloat16)
            for r in range(reps):
                rhs = wv[pl.ds(c * 2, 2), r].reshape(256, 128)
                cc[r, at, :] = jnp.dot(lhs, rhs, preferred_element_type=jnp.float32)
            return carry

        lax.fori_loop(0, cols, product, 0, unroll=8)
        high, rest = [], []
        for step in chunk:
            value = jnp.concatenate(
                [cc[r, pl.ds(step, blocks, stride=STEPS), :] for r in range(reps)], axis=0
            )
            top = value.astype(jnp.bfloat16)
            high.append(top)
            rest.append((value - top.astype(jnp.float32)).astype(jnp.bfloat16))
        both = jnp.concatenate(
            [jnp.concatenate(high, axis=1), jnp.concatenate(rest, axis=1)], axis=0
        )
        sums = jnp.dot(sel[...], both, preferred_element_type=jnp.float32)
        for m in range(INNER):
            for i in range(len(chunk)):
                s1[m, k, i] = sums[
                    m * groups * TB : (m + 1) * groups * TB, i * 128 : (i + 1) * 128
                ]
        for copy in inner_copies[k]:
            copy.start()
        if k > 0:
            second_phase(k - 1)
    second_phase(len(CHUNKS) - 1)
    for k, chunk in enumerate(CHUNKS):
        for copy in outer_copies[k]:
            copy.wait_recv()
        total = s2[group, k]
        for d in range(1, groups):
            total = total + r2[d - 1, k]
        for i, step in enumerate(chunk):
            out_ref[:, step, :] = total[i]
    for k in range(len(CHUNKS)):
        for copy in inner_copies[k] + outer_copies[k]:
            copy.wait_send()
    fin_copy.wait()


def on_device(n, initial, depth_field, coriolis, cell_area, face_len, owners, offsets, weights):
    cols, ny = depth_field.shape
    ext = cols + 2 * HALO
    blocks, reps = owners.shape
    groups = n // INNER
    chunks = len(CHUNKS)
    size = len(CHUNKS[0])
    f32 = jnp.float32
    anywhere = pl.BlockSpec(memory_space=pl.ANY)
    vmem = pl.BlockSpec(memory_space=pltpu.VMEM)
    dma = pltpu.SemaphoreType.DMA
    return pl.pallas_call(
        functools.partial(kernel, n),
        out_shape=(
            jax.ShapeDtypeStruct((TB, STEPS, 128), f32),
            jax.ShapeDtypeStruct(initial.shape, f32),
        ),
        in_specs=[anywhere] * 5 + [vmem] * 2 + [anywhere],
        out_specs=(vmem, anywhere),
        scratch_shapes=[
            pltpu.VMEM((8, ext, ny), f32),
            pltpu.VMEM(weights.shape, jnp.bfloat16),
            pltpu.VMEM((2, 4, 8, ny), f32),
            pltpu.VMEM((2, 4, 8, ny), f32),
            pltpu.VMEM((2, cols * 8, 128), f32),
            pltpu.VMEM((reps, cols * 8, 128), f32),
            pltpu.VMEM((n * TB, 2 * blocks * reps), jnp.bfloat16),
            pltpu.VMEM((INNER, chunks, size, groups * TB, 128), f32),
            pltpu.VMEM((INNER - 1, chunks, size, groups * TB, 128), f32),
            pltpu.VMEM((groups, chunks, size, TB, 128), f32),
            pltpu.VMEM((groups - 1, chunks, size, TB, 128), f32),
            dma((5,)),
            dma((WEIGHT_PARTS,)),
            dma((2,)),
            dma((2,)),
            dma((INNER - 1, chunks)),
            dma((INNER - 1, chunks)),
            dma((groups - 1, chunks)),
            dma((groups - 1, chunks)),
            dma,
        ],
        compiler_params=pltpu.CompilerParams(
            collective_id=0, has_side_effects=True, vmem_limit_bytes=40 * 1024 * 1024
        ),
        cost_estimate=pl.CostEstimate(
            flops=2 * weights.size * STEPS, bytes_accessed=2 * weights.size, transcendentals=0
        ),
    )(initial, depth_field, coriolis, cell_area, face_len, owners, offsets, weights)


def solution(mesh):
    columns = ("exp", "tile")
    placed = (
        P(None, columns, None),
        P(columns, None),
        P(columns, None),
        P(columns, None),
        P(None, columns, None),
        P(columns, None),
        P(columns, None),
        P(columns, None, None, None),
    )
    return jax.shard_map(
        functools.partial(on_device, mesh.shape["tile"]),
        mesh=mesh,
        in_specs=placed,
        out_specs=(P(columns, None, None), P(None, columns, None)),
        check_vma=False,
    )
```

time: 145 us -> 33.6 us (0.23)
  waiting for transfers between devices: 80.8 us -> 0 us
  starting transfers between devices: 26.3 us -> 0 us
  Pallas kernels: 0 us -> 23.5 us
  between operations: 14.2 us -> 0.65 us
  other arithmetic: 11.1 us -> 0 us
  matrix products: 4.04 us -> 0 us
  local copies, waits for them, and re-layouts: 6.98 us -> 8.98 us
    reduce_scatter x1 -> x0, waiting for transfers between devices: 77.5 us -> none  [on_device(): lax.psum_scatter(jnp.dot(select, flat, precision=lax.Precision.HIGHEST, p...]
    ppermute x10 -> x0, starting transfers between devices: 26.2 us -> none  [the longest x5 23 us: with_halo(): lax.ppermute(head, axis, [((i + 1) % count, i) for i in range(count)])]
    pallas_call x0 -> x1, Pallas kernels: none -> 23.5 us  [on_device(): pl.pallas_call(functools.partial(kernel, n), out_shape=(jax.ShapeDtypeStr...]
    unnamed x9 -> x16, local copies, waits for them, and re-layouts: 0.93 us -> 8.98 us
    mul x17 -> x0, other arithmetic: 6.73 us -> none  [the longest x4 1.95 us: advance(): own_n * (0.5 * (own_h + above_h) - 0.5 * wave_y * (above_v - own_v))]
    slice x20 -> x0, local copies, waits for them, and re-layouts: 4.33 us -> none  [the longest x1 0.83 us: advance(): above_d = jnp.concatenate([own_d[:, 1:], own_d[:, -1:]], axis=1)]
    dot_general x2 -> x0, matrix products: 4.04 us -> none  [the longest x1 2.87 us: on_device(): jnp.einsum('sbk,brkt->brst', snapped, weights, preferred_element_type=jnp...]
    ppermute x10 -> x0, waiting for transfers between devices: 3.26 us -> none  [the longest x5 3.25 us: with_halo(): lax.ppermute(tail, axis, [(i, (i + 1) % count) for i in range(count)])]
  transfers between devices with their start and end apart: 11 -> 0, of which waited for: 4 -> 0; matrix products, arithmetic and copies ran while one was open for 7% -> 0% of each run, Pallas kernels for 0% -> 0%
where the time goes in v1:
time: 33.6 us; the launch traced here: 33.1 us
  Pallas kernels  23.5 us (70%)
  local copies, waits for them, and re-layouts  8.98 us (27%)
  between operations  0.65 us (2%)
    pallas_call x1, Pallas kernels, on_device(): pl.pallas_call(functools.partial(kernel, n), out_shape=(jax.ShapeDtypeStr...  23.5 us
    unnamed x16, local copies, waits for them, and re-layouts  8.98 us

profile of v1, /device:TPU:0, one launch (start us, length us, event | category | flops | bytes accessed | tf_op | source)
XLA Modules:
  0.0 33.1 jit_solution(6443490797493956886)
XLA Ops:
  0.6 0.8 %copy.10.own_ref = s32[64,2]{1,0:T(8,128)S(1)} copy(s32[64,2]{0,1:T(2,128)} %param.13) | data formatting | bytes 1024 | tf_op args[5]
  1.4 0.8 %copy.11.off_ref = s32[64,2]{1,0:T(8,128)S(1)} copy(s32[64,2]{0,1:T(2,128)} %param.14) | data formatting | bytes 1024 | tf_op args[6]
  2.2 0.0 copy-start
  2.2 2.2 %copy-done = bf16[64,2,128,128]{3,2,1,0:T(8,128)(2,1)S(1)} copy-done((bf16[64,2,128,128]{3,2,1,0:T(8,128)(2,1)S(1)}, bf16[64,2,128,128]{3,2,1,0:T(8,128)(2,1)}, u32[]{:S(2)}) %copy-start) | copy-done | bytes 4194328
  4.4 0.0 copy-start.1
  4.4 0.9 %copy-done.1 = f32[3,32,256]{2,1,0:T(8,128)S(1)} copy-done((f32[3,32,256]{2,1,0:T(8,128)S(1)}, f32[3,32,256]{2,1,0:T(8,128)}, u32[]{:S(2)}) %copy-start.1) | copy-done | bytes 98328
  5.2 0.0 copy-start.2
  5.2 0.8 %copy-done.2 = f32[2,32,256]{2,1,0:T(8,128)S(1)} copy-done((f32[2,32,256]{2,1,0:T(8,128)S(1)}, f32[2,32,256]{2,1,0:T(8,128)}, u32[]{:S(2)}) %copy-start.2) | copy-done | bytes 65560
  6.1 0.0 copy-start.3
  6.1 0.8 %copy-done.3 = f32[32,256]{1,0:T(8,128)S(1)} copy-done((f32[32,256]{1,0:T(8,128)S(1)}, f32[32,256]{1,0:T(8,128)}, u32[]{:S(2)}) %copy-start.3) | copy-done | bytes 32792
  6.8 0.0 copy-start.4
  6.8 0.8 %copy-done.4 = f32[32,256]{1,0:T(8,128)S(1)} copy-done((f32[32,256]{1,0:T(8,128)S(1)}, f32[32,256]{1,0:T(8,128)}, u32[]{:S(2)}) %copy-start.4) | copy-done | bytes 32792
  7.6 0.0 copy-start.5
  7.6 0.8 %copy-done.5 = f32[32,256]{1,0:T(8,128)S(1)} copy-done((f32[32,256]{1,0:T(8,128)S(1)}, f32[32,256]{1,0:T(8,128)}, u32[]{:S(2)}) %copy-start.5) | copy-done | bytes 32792
  8.4 23.5 %shard_map.95 = (f32[16,4,128]{2,1,0:T(4,128)S(1)}, f32[3,32,256]{2,1,0:T(8,128)S(1)}) custom-call(f32[3,32,256]{2,1,0:T(8,128)S(1)} %copy-done.1, f32[32,256]{1,0:T(8,128)S(1)} %copy-done.3, f32[32,256]{1,0:T(8,128)S(1)} %copy-done.4, f32[32,256]{1,0:T(8,128)S(1)} %copy-done.5, f32[2,32,256]{2,1,0:T(8,128)S(1)} %copy-done.2, s32[64,2]{1,0:T(8,128)S(1)} %copy.10.own_ref, ...), custom_call_target="tpu_custom_call" | custom-call | flops 16777216 | bytes 4194304 | tf_op jit(solution)/shard_map/pallas_call | solution.py:296
  31.9 0.6 %copy.14 = f32[16,4,128]{2,1,0:T(4,128)} copy(f32[16,4,128]{2,1,0:T(4,128)S(1)} %get-tuple-element.4) | data formatting | bytes 65536
  32.5 0.6 %copy.15 = f32[3,32,256]{2,1,0:T(8,128)} copy(f32[3,32,256]{2,1,0:T(8,128)S(1)} %get-tuple-element.5) | data formatting | bytes 196608
Async XLA Ops:
  2.2 2.2 %copy-start = (bf16[64,2,128,128]{3,2,1,0:T(8,128)(2,1)S(1)}, bf16[64,2,128,128]{3,2,1,0:T(8,128)(2,1)}, u32[]{:S(2)}) copy-start(bf16[64,2,128,128]{3,2,1,0:T(8,128)(2,1)} %w_ref.1) | copy-start | bytes 12582916
  4.4 0.9 %copy-start.1 = (f32[3,32,256]{2,1,0:T(8,128)S(1)}, f32[3,32,256]{2,1,0:T(8,128)}, u32[]{:S(2)}) copy-start(f32[3,32,256]{2,1,0:T(8,128)} %init_ref.1) | copy-start | bytes 294916
  5.2 0.8 %copy-start.2 = (f32[2,32,256]{2,1,0:T(8,128)S(1)}, f32[2,32,256]{2,1,0:T(8,128)}, u32[]{:S(2)}) copy-start(f32[2,32,256]{2,1,0:T(8,128)} %face_ref.1) | copy-start | bytes 196612
  6.1 0.8 %copy-start.3 = (f32[32,256]{1,0:T(8,128)S(1)}, f32[32,256]{1,0:T(8,128)}, u32[]{:S(2)}) copy-start(f32[32,256]{1,0:T(8,128)} %depth_ref.1) | copy-start | bytes 98308
  6.8 0.8 %copy-start.4 = (f32[32,256]{1,0:T(8,128)S(1)}, f32[32,256]{1,0:T(8,128)}, u32[]{:S(2)}) copy-start(f32[32,256]{1,0:T(8,128)} %cor_ref.1) | copy-start | bytes 98308
  7.6 0.8 %copy-start.5 = (f32[32,256]{1,0:T(8,128)S(1)}, f32[32,256]{1,0:T(8,128)}, u32[]{:S(2)}) copy-start(f32[32,256]{1,0:T(8,128)} %area_ref.1) | copy-start | bytes 98308

commit v2 on v1

v2 whole, which is shorter than its diff:
```python
import functools

import jax
import jax.numpy as jnp
from jax import lax
from jax.experimental import pallas as pl
from jax.experimental.pallas import tpu as pltpu
from jax.sharding import PartitionSpec as P

STEPS = 4
TB = 16
TIME_STEP = 0.3
INNER = 4
HALO = 4
WEIGHT_PARTS = 4
MESH = pl.DeviceIdType.MESH


def kernel(
    n,
    init_ref,
    depth_ref,
    cor_ref,
    area_ref,
    face_ref,
    own_hbm,
    off_hbm,
    w_ref,
    out_ref,
    fin_ref,
    st,
    own_ref,
    off_ref,
    wv,
    hs,
    hr,
    sd,
    cc,
    sel,
    plane_out,
    plane_in,
    line_out,
    line_in,
    line_out_b,
    line_in_b,
    plane_out_b,
    plane_in_b,
    load_sem,
    w_sem,
    hs_sem,
    hr_sem,
    plane_sems,
    line_sems,
    line_sems_b,
    plane_sems_b,
):
    cols = init_ref.shape[1]
    ny = init_ref.shape[2]
    blocks = w_ref.shape[0]
    reps = w_ref.shape[1]
    groups = n // INNER
    rows = n * TB
    me = lax.axis_index("tile")
    mine = lax.rem(me, INNER)
    group = me // INNER
    left = lax.rem(me + n - 1, n)
    right = lax.rem(me + 1, n)
    mates = [mine + 1 - 2 * lax.rem(mine, 2), lax.rem(mine + 2, INNER), INNER - 1 - mine]
    peers = [lax.rem(group + d, groups) for d in range(1, groups)]
    mate_ids = [group * INNER + m for m in mates]
    peer_ids = [g * INNER + mine for g in peers]

    loads = [
        pltpu.make_async_copy(init_ref, st.at[pl.ds(0, 3)], load_sem.at[0]),
        pltpu.make_async_copy(depth_ref, st.at[3], load_sem.at[1]),
        pltpu.make_async_copy(cor_ref, st.at[4], load_sem.at[2]),
        pltpu.make_async_copy(area_ref, st.at[5], load_sem.at[3]),
        pltpu.make_async_copy(face_ref, st.at[pl.ds(6, 2)], load_sem.at[4]),
    ]
    index_loads = [
        pltpu.make_async_copy(own_hbm, own_ref, load_sem.at[5]),
        pltpu.make_async_copy(off_hbm, off_ref, load_sem.at[6]),
    ]
    for copy in loads + index_loads:
        copy.start()
    part = blocks // WEIGHT_PARTS
    w_loads = [
        pltpu.make_async_copy(
            w_ref.at[pl.ds(i * part, part)], wv.at[pl.ds(i * part, part)], w_sem.at[i]
        )
        for i in range(WEIGHT_PARTS)
    ]
    barrier = pltpu.get_barrier_semaphore()
    partners = [left, right] + mate_ids + peer_ids
    for partner in partners:
        pl.semaphore_signal(barrier, inc=1, device_id={"tile": partner}, device_id_type=MESH)
    for copy in w_loads:
        copy.start()
    for copy in loads:
        copy.wait()

    def remote(src, dst, send, recv, to):
        return pltpu.make_async_remote_copy(
            src_ref=src,
            dst_ref=dst,
            send_sem=send,
            recv_sem=recv,
            device_id={"tile": to},
            device_id_type=MESH,
        )

    low = lax.broadcasted_iota(jnp.int32, (8, ny), 0) < HALO
    for a in range(4):
        even, odd = st[2 * a, 0:8, :], st[2 * a + 1, 0:8, :]
        hs[0, a] = jnp.where(low, even, pltpu.roll(odd, HALO, 0))
        even, odd = st[2 * a, cols - 8 : cols, :], st[2 * a + 1, cols - 8 : cols, :]
        hs[1, a] = jnp.where(low, pltpu.roll(odd, HALO, 0), even)
    pl.semaphore_wait(barrier, len(partners))
    halos = [
        remote(hs.at[i], hr.at[i], hs_sem.at[i], hr_sem.at[i], to)
        for i, to in enumerate((left, right))
    ]
    for copy in halos:
        copy.start()

    def run(fields, keep):
        h, u, v, depth, turn, factor, half_x, n_len = fields
        count = h.shape[0]

        def east(x):
            return pltpu.roll(x, count - 1, 0)

        def west(x):
            return pltpu.roll(x, 1, 0)

        def north(x):
            return pltpu.roll(x, ny - 1, 1)

        def south(x):
            return pltpu.roll(x, 1, 1)

        lane = lax.broadcasted_iota(jnp.int32, (count, ny), 1)
        first, last = lane == 0, lane == ny - 1
        turn = TIME_STEP * turn
        factor = TIME_STEP / factor
        half_x = 0.5 * half_x
        wave_x = half_x * jnp.sqrt(jnp.maximum(depth, east(depth)))
        half_y = jnp.where(last, 0.0, 0.5 * n_len)
        wave_y = half_y * jnp.sqrt(jnp.maximum(depth, north(depth)))
        wall_h = jnp.where(first, -n_len, jnp.where(last, n_len, 0.0))
        wall_v = jnp.where(first | last, n_len * jnp.sqrt(depth), 0.0)
        for step in range(STEPS):
            q = depth * u
            he, ue, ve = east(h), east(u), east(v)
            fh = half_x * (q + east(q)) - wave_x * (he - h)
            fu = half_x * (h + he) - wave_x * (ue - u)
            fv = wave_x * (v - ve)
            p = depth * v
            hn, un, vn = north(h), north(u), north(v)
            gh = half_y * (p + north(p)) - wave_y * (hn - h)
            gu = wave_y * (u - un)
            gv = half_y * (h + hn) - wave_y * (vn - v)
            new_h = h - factor * (fh - west(fh) + gh - south(gh))
            new_u = u - factor * (fu - west(fu) + gu - south(gu)) + turn * v
            new_v = (
                v - factor * (fv - west(fv) + gv - south(gv) + wall_h * h + wall_v * v) - turn * u
            )
            h, u, v = new_h, new_u, new_v
            keep(step, h)
        return h, u, v

    def product(c, carry):
        at = pl.ds(pl.multiple_of(c * 8, 8), 8)
        lhs = jnp.concatenate([sd[0, at, :], sd[1, at, :]], axis=1).astype(jnp.bfloat16)
        for r in range(reps):
            rhs = wv[pl.ds(c * 2, 2), r].reshape(256, 128)
            cc[r, at, :] = jnp.dot(lhs, rhs, preferred_element_type=jnp.float32)
        return carry

    for copy in index_loads:
        copy.wait()
    sd[...] = jnp.zeros_like(sd)
    owner = own_ref[...]
    target = (owner % INNER) * (groups * TB) + (owner // INNER) * TB + off_ref[...]
    place = lax.broadcasted_iota(jnp.int32, (rows, blocks), 0)
    hot = jnp.concatenate(
        [jnp.where(place == target[r : r + 1, :], 1.0, 0.0) for r in range(reps)], axis=1
    ).astype(jnp.bfloat16)
    sel[...] = jnp.concatenate([hot, hot], axis=1)

    def keep_inside(step, h):
        sd[0, pl.ds(step, cols, stride=8), :] = h[:, :128]
        sd[1, pl.ds(STEPS + step, cols, stride=8), :] = h[:, 128:]

    inside = run([st[q] for q in range(8)], keep_inside)
    for q in range(3):
        fin_ref[q] = inside[q]
    for copy in w_loads:
        copy.wait()
    lax.fori_loop(HALO, cols - HALO, product, 0, unroll=8)

    for copy in halos:
        copy.wait()
    edge = []
    for a in range(4):
        after, before = hr[0, a], hr[1, a]
        even = jnp.where(low, after, before)
        odd = jnp.where(low, pltpu.roll(after, HALO, 0), pltpu.roll(before, HALO, 0))
        for q, value in ((2 * a, even), (2 * a + 1, odd)):
            edge.append(
                jnp.concatenate([st[q, cols - 8 : cols, :], value, st[q, 0:8, :]], axis=0)
            )

    def keep_edge(step, h):
        for begin, source in ((0, 16), (cols - HALO, 4)):
            part = h[source : source + HALO]
            sd[0, pl.ds(begin * 8 + step, HALO, stride=8), :] = part[:, :128]
            sd[1, pl.ds(begin * 8 + STEPS + step, HALO, stride=8), :] = part[:, 128:]

    edge = run(edge, keep_edge)
    for c in range(HALO):
        product(c, 0)
        product(cols - HALO + c, 0)

    high, rest = [], []
    for step in range(STEPS):
        value = jnp.concatenate(
            [cc[r, pl.ds(step, blocks, stride=STEPS), :] for r in range(reps)], axis=0
        )
        top = value.astype(jnp.bfloat16)
        high.append(top)
        rest.append((value - top.astype(jnp.float32)).astype(jnp.bfloat16))
    both = jnp.concatenate([jnp.concatenate(high, axis=1), jnp.concatenate(rest, axis=1)], axis=0)
    sums = jnp.dot(sel[...], both, preferred_element_type=jnp.float32)
    for g in range(groups):
        for m in range(INNER):
            at = (m * groups + g) * TB
            line_out_b[g, m] = sums[at : at + TB, :128]
    line_b = [
        remote(line_out_b.at[g], line_in_b.at[d], line_sems_b.at[0, d], line_sems_b.at[1, d], to)
        for d, (g, to) in enumerate(zip(peers, peer_ids))
    ]
    for copy in line_b:
        copy.start()
    for m in range(INNER):
        for i in range(STEPS - 1):
            plane_out[m, i] = sums[
                m * groups * TB : (m + 1) * groups * TB, (i + 1) * 128 : (i + 2) * 128
            ].reshape(groups, TB, 128)
    plane = [
        remote(plane_out.at[m], plane_in.at[d], plane_sems.at[0, d], plane_sems.at[1, d], to)
        for d, (m, to) in enumerate(zip(mates, mate_ids))
    ]
    for copy in reversed(plane):
        copy.start()

    for q in range(3):
        fin_ref[q, 0:HALO, :] = edge[q][16 : 16 + HALO]
        fin_ref[q, cols - HALO : cols, :] = edge[q][4 : 4 + HALO]

    for copy in line_b:
        copy.wait_recv()
    total = line_out_b[group]
    for d in range(groups - 1):
        total = total + line_in_b[d]
    plane_out_b[...] = total
    plane_b = [
        remote(
            plane_out_b.at[m], plane_in_b.at[d], plane_sems_b.at[0, d], plane_sems_b.at[1, d], to
        )
        for d, (m, to) in enumerate(zip(mates, mate_ids))
    ]
    for copy in plane_b:
        copy.start()

    for copy in plane:
        copy.wait_recv()
    for g in range(groups):
        total = plane_out[mine, :, g]
        for d in range(INNER - 1):
            total = total + plane_in[d, :, g]
        line_out[g] = total
    line = [
        remote(line_out.at[g], line_in.at[d], line_sems.at[0, d], line_sems.at[1, d], to)
        for d, (g, to) in enumerate(zip(peers, peer_ids))
    ]
    for copy in line:
        copy.start()

    for copy in plane_b:
        copy.wait_recv()
    total = plane_out_b[mine]
    for d in range(INNER - 1):
        total = total + plane_in_b[d]
    out_ref[:, 0, :] = total
    for copy in line:
        copy.wait_recv()
    total = line_out[group]
    for d in range(groups - 1):
        total = total + line_in[d]
    for i in range(STEPS - 1):
        out_ref[:, i + 1, :] = total[i]
    for copy in plane + line + plane_b + line_b:
        copy.wait_send()


def on_device(n, initial, depth_field, coriolis, cell_area, face_len, owners, offsets, weights):
    cols, ny = depth_field.shape
    blocks, reps = owners.shape
    groups = n // INNER
    f32 = jnp.float32
    hbm = pl.BlockSpec(memory_space=pltpu.HBM)
    vmem = pl.BlockSpec(memory_space=pltpu.VMEM)
    dma = pltpu.SemaphoreType.DMA
    return pl.pallas_call(
        functools.partial(kernel, n),
        out_shape=(
            jax.ShapeDtypeStruct((TB, STEPS, 128), f32),
            jax.ShapeDtypeStruct(initial.shape, f32),
        ),
        in_specs=[hbm] * 8,
        out_specs=(vmem, vmem),
        scratch_shapes=[
            pltpu.VMEM((8, cols, ny), f32),
            pltpu.VMEM((reps, blocks), jnp.int32),
            pltpu.VMEM((reps, blocks), jnp.int32),
            pltpu.VMEM(weights.shape, jnp.bfloat16),
            pltpu.VMEM((2, 4, 8, ny), f32),
            pltpu.VMEM((2, 4, 8, ny), f32),
            pltpu.VMEM((2, cols * 8, 128), f32),
            pltpu.VMEM((reps, cols * 8, 128), f32),
            pltpu.VMEM((n * TB, 2 * blocks * reps), jnp.bfloat16),
            pltpu.VMEM((INNER, STEPS - 1, groups, TB, 128), f32),
            pltpu.VMEM((INNER - 1, STEPS - 1, groups, TB, 128), f32),
            pltpu.VMEM((groups, STEPS - 1, TB, 128), f32),
            pltpu.VMEM((groups - 1, STEPS - 1, TB, 128), f32),
            pltpu.VMEM((groups, INNER, TB, 128), f32),
            pltpu.VMEM((groups - 1, INNER, TB, 128), f32),
            pltpu.VMEM((INNER, TB, 128), f32),
            pltpu.VMEM((INNER - 1, TB, 128), f32),
            dma((7,)),
            dma((WEIGHT_PARTS,)),
            dma((2,)),
            dma((2,)),
            dma((2, INNER - 1)),
            dma((2, groups - 1)),
            dma((2, groups - 1)),
            dma((2, INNER - 1)),
        ],
        compiler_params=pltpu.CompilerParams(
            collective_id=0, has_side_effects=True, vmem_limit_bytes=60 * 1024 * 1024
        ),
        cost_estimate=pl.CostEstimate(
            flops=2 * weights.size * STEPS, bytes_accessed=2 * weights.size, transcendentals=0
        ),
    )(initial, depth_field, coriolis, cell_area, face_len, owners.T, offsets.T, weights)


def solution(mesh):
    columns = ("exp", "tile")
    placed = (
        P(None, columns, None),
        P(columns, None),
        P(columns, None),
        P(columns, None),
        P(None, columns, None),
        P(columns, None),
        P(columns, None),
        P(columns, None, None, None),
    )
    return jax.shard_map(
        functools.partial(on_device, mesh.shape["tile"]),
        mesh=mesh,
        in_specs=placed,
        out_specs=(P(columns, None, None), P(None, columns, None)),
        check_vma=False,
    )
```

time: 33.6 us -> 25.7 us (0.76)
  local copies, waits for them, and re-layouts: 8.98 us -> 2.91 us
  Pallas kernels: 23.5 us -> 21.9 us
    unnamed x16 -> x2, local copies, waits for them, and re-layouts: 8.98 us -> 2.91 us
    pallas_call x1, Pallas kernels: 23.5 us -> 21.9 us  [on_device(): pl.pallas_call(functools.partial(kernel, n), out_shape=(jax.ShapeDtypeStr...]
where the time goes in v2:
time: 25.7 us; the launch traced here: 25.5 us
  Pallas kernels  21.9 us (85%)
  local copies, waits for them, and re-layouts  2.91 us (11%)
  between operations  0.64 us (2%)
    pallas_call x1, Pallas kernels, on_device(): pl.pallas_call(functools.partial(kernel, n), out_shape=(jax.ShapeDtypeStr...  21.9 us
    unnamed x2, local copies, waits for them, and re-layouts  2.91 us

profile of v2, /device:TPU:0, one launch (start us, length us, event | category | flops | bytes accessed | tf_op | source)
XLA Modules:
  0.0 25.5 jit_solution(13058356763390393368)
XLA Ops:
  0.6 21.9 %shard_map.95 = (f32[16,4,128]{2,1,0:T(4,128)}, f32[3,32,256]{2,1,0:T(8,128)}) custom-call(f32[3,32,256]{2,1,0:T(8,128)} %init_ref.1, f32[32,256]{1,0:T(8,128)} %depth_ref.1, f32[32,256]{1,0:T(8,128)} %cor_ref.1, f32[32,256]{1,0:T(8,128)} %area_ref.1, f32[2,32,256]{2,1,0:T(8,128)} %face_ref.1, s32[2,64]{1,0:T(2,128)} %bitcast.2, s32[2,64]{1,0:T(2,128)} %bitcast.3, ...), custom_call_target="tpu_custom_call" | custom-call | flops 16777216 | bytes 4194304 | tf_op jit(solution)/shard_map/pallas_call | solution.py:315
  22.5 1.4 %copy.12 = f32[16,4,128]{2,1,0:T(4,128)} copy(f32[16,4,128]{2,1,0:T(4,128)} %get-tuple-element.4) | data formatting | bytes 65536
  23.9 1.5 %copy.13 = f32[3,32,256]{2,1,0:T(8,128)} copy(f32[3,32,256]{2,1,0:T(8,128)} %get-tuple-element.5) | data formatting | bytes 196608

commit v3 on v2

--- a/solution.py
+++ b/solution.py
@@ -304,6 +304,17 @@
         copy.wait_send()
 
 
+def store(sum_ref, last_ref, out_ref, fin_ref, sems):
+    copies = [
+        pltpu.make_async_copy(sum_ref, out_ref, sems.at[0]),
+        pltpu.make_async_copy(last_ref, fin_ref, sems.at[1]),
+    ]
+    for copy in copies:
+        copy.start()
+    for copy in copies:
+        copy.wait()
+
+
 def on_device(n, initial, depth_field, coriolis, cell_area, face_len, owners, offsets, weights):
     cols, ny = depth_field.shape
     blocks, reps = owners.shape
@@ -312,11 +323,11 @@
     hbm = pl.BlockSpec(memory_space=pltpu.HBM)
     vmem = pl.BlockSpec(memory_space=pltpu.VMEM)
     dma = pltpu.SemaphoreType.DMA
-    return pl.pallas_call(
+    sums, last = pl.pallas_call(
         functools.partial(kernel, n),
         out_shape=(
-            jax.ShapeDtypeStruct((TB, STEPS, 128), f32),
-            jax.ShapeDtypeStruct(initial.shape, f32),
+            pltpu.VMEM((TB, STEPS, 128), f32),
+            pltpu.VMEM(initial.shape, f32),
         ),
         in_specs=[hbm] * 8,
         out_specs=(vmem, vmem),
@@ -348,12 +359,25 @@
             dma((2, INNER - 1)),
         ],
         compiler_params=pltpu.CompilerParams(
-            collective_id=0, has_side_effects=True, vmem_limit_bytes=60 * 1024 * 1024
+            collective_id=0, has_side_effects=True, vmem_limit_bytes=40 * 1024 * 1024
         ),
         cost_estimate=pl.CostEstimate(
             flops=2 * weights.size * STEPS, bytes_accessed=2 * weights.size, transcendentals=0
         ),
-    )(initial, depth_field, coriolis, cell_area, face_len, owners.T, offsets.T, weights)
+    )(*[pltpu.with_memory_space_constraint(x, pltpu.HBM) for x in (initial, depth_field, coriolis, cell_area, face_len, owners.T, offsets.T, weights)])
+    return pl.pallas_call(
+        store,
+        out_shape=(
+            jax.ShapeDtypeStruct(sums.shape, f32),
+            jax.ShapeDtypeStruct(last.shape, f32),
+        ),
+        in_specs=[vmem, vmem],
+        out_specs=(hbm, hbm),
+        scratch_shapes=[dma((2,))],
+    )(
+        pltpu.with_memory_space_constraint(sums, pltpu.VMEM),
+        pltpu.with_memory_space_constraint(last, pltpu.VMEM),
+    )
 
 
 def solution(mesh):

time: 25.7 us -> 22.7 us (0.88)
  local copies, waits for them, and re-layouts: 2.91 us -> 0 us
    unnamed x2 -> x0, local copies, waits for them, and re-layouts: 2.91 us -> none
    pallas_call x1 -> x2, Pallas kernels: 21.9 us -> 21.9 us  [the longest x1 21.3 us: on_device(): pl.pallas_call(functools.partial(kernel, n), out_shape=(pltpu.VMEM((TB, S...]
where the time goes in v3:
time: 22.7 us; the launch traced here: 22.6 us
  Pallas kernels  21.9 us (96%)
  between operations  0.64 us (3%)
    pallas_call x1, Pallas kernels, on_device(): pl.pallas_call(functools.partial(kernel, n), out_shape=(pltpu.VMEM((TB, S...  21.3 us
    pallas_call x1, Pallas kernels, on_device(): pl.pallas_call(store, out_shape=(jax.ShapeDtypeStruct(sums.shape, f32), j...  0.67 us

profile of v3, /device:TPU:0, one launch (start us, length us, event | category | flops | bytes accessed | tf_op | source)
XLA Modules:
  0.0 22.6 jit_solution(9195276990985132275)
XLA Ops:
  0.6 21.3 %shard_map.95 = (f32[16,4,128]{2,1,0:T(4,128)S(1)}, f32[3,32,256]{2,1,0:T(8,128)S(1)}) custom-call(f32[3,32,256]{2,1,0:T(8,128)} %init_ref.1, f32[32,256]{1,0:T(8,128)} %depth_ref.1, f32[32,256]{1,0:T(8,128)} %cor_ref.1, f32[32,256]{1,0:T(8,128)} %area_ref.1, f32[2,32,256]{2,1,0:T(8,128)} %face_ref.1, s32[2,64]{1,0:T(2,128)} %bitcast.2, s32[2,64]{1,0:T(2,128)} %bitcast.3, ...), custom_call_target="tpu_custom_call" | custom-call | flops 16777216 | bytes 4194304 | tf_op jit(solution)/shard_map/pallas_call | solution.py:326
  21.9 0.7 %shard_map.96 = (f32[16,4,128]{2,1,0:T(4,128)}, f32[3,32,256]{2,1,0:T(8,128)}) custom-call(f32[16,4,128]{2,1,0:T(4,128)S(1)} %get-tuple-element.4.sum_ref, f32[3,32,256]{2,1,0:T(8,128)S(1)} %get-tuple-element.5.last_ref), custom_call_target="tpu_custom_call" | custom-call | tf_op jit(solution)/shard_map/pallas_call | solution.py:368

commit v4 on v3

--- a/solution.py
+++ b/solution.py
@@ -231,28 +231,29 @@
         high.append(top)
         rest.append((value - top.astype(jnp.float32)).astype(jnp.bfloat16))
     both = jnp.concatenate([jnp.concatenate(high, axis=1), jnp.concatenate(rest, axis=1)], axis=0)
-    sums = jnp.dot(sel[...], both, preferred_element_type=jnp.float32)
+    sums = jnp.dot(sel[...], both[:, :128], preferred_element_type=jnp.float32)
     for g in range(groups):
         for m in range(INNER):
             at = (m * groups + g) * TB
-            line_out_b[g, m] = sums[at : at + TB, :128]
+            line_out_b[g, m] = sums[at : at + TB]
     line_b = [
         remote(line_out_b.at[g], line_in_b.at[d], line_sems_b.at[0, d], line_sems_b.at[1, d], to)
         for d, (g, to) in enumerate(zip(peers, peer_ids))
     ]
     for copy in line_b:
         copy.start()
-    for m in range(INNER):
-        for i in range(STEPS - 1):
-            plane_out[m, i] = sums[
-                m * groups * TB : (m + 1) * groups * TB, (i + 1) * 128 : (i + 2) * 128
-            ].reshape(groups, TB, 128)
     plane = [
         remote(plane_out.at[m], plane_in.at[d], plane_sems.at[0, d], plane_sems.at[1, d], to)
         for d, (m, to) in enumerate(zip(mates, mate_ids))
     ]
-    for copy in reversed(plane):
-        copy.start()
+    share = groups * TB
+    for m, copy in zip(mates[::-1] + [mine], plane[::-1] + [None]):
+        chosen = sel[pl.ds(pl.multiple_of(m * share, share), share), :]
+        sums = jnp.dot(chosen, both[:, 128:], preferred_element_type=jnp.float32)
+        for i in range(STEPS - 1):
+            plane_out[m, i] = sums[:, i * 128 : (i + 1) * 128].reshape(groups, TB, 128)
+        if copy is not None:
+            copy.start()
 
     for q in range(3):
         fin_ref[q, 0:HALO, :] = edge[q][16 : 16 + HALO]
@@ -275,17 +276,17 @@
 
     for copy in plane:
         copy.wait_recv()
-    for g in range(groups):
+    line = [
+        remote(line_out.at[g], line_in.at[d], line_sems.at[0, d], line_sems.at[1, d], to)
+        for d, (g, to) in enumerate(zip(peers, peer_ids))
+    ]
+    for g, copy in zip(peers + [group], line + [None]):
         total = plane_out[mine, :, g]
         for d in range(INNER - 1):
             total = total + plane_in[d, :, g]
         line_out[g] = total
-    line = [
-        remote(line_out.at[g], line_in.at[d], line_sems.at[0, d], line_sems.at[1, d], to)
-        for d, (g, to) in enumerate(zip(peers, peer_ids))
-    ]
-    for copy in line:
-        copy.start()
+        if copy is not None:
+            copy.start()
 
     for copy in plane_b:
         copy.wait_recv()

time: 22.7 us -> 22.8 us (level)
  no operation moved by 1% of the time
where the time goes in v4:
time: 22.8 us; the launch traced here: 22.6 us
  Pallas kernels  22 us (96%)
  between operations  0.64 us (3%)
    pallas_call x1, Pallas kernels, on_device(): pl.pallas_call(functools.partial(kernel, n), out_shape=(pltpu.VMEM((TB, S...  21.3 us
    pallas_call x1, Pallas kernels, on_device(): pl.pallas_call(store, out_shape=(jax.ShapeDtypeStruct(sums.shape, f32), j...  0.67 us

profile of v4, /device:TPU:0, one launch (start us, length us, event | category | flops | bytes accessed | tf_op | source)
XLA Modules:
  0.0 22.6 jit_solution(2302724570383995063)
XLA Ops:
  0.6 21.3 %shard_map.95 = (f32[16,4,128]{2,1,0:T(4,128)S(1)}, f32[3,32,256]{2,1,0:T(8,128)S(1)}) custom-call(f32[3,32,256]{2,1,0:T(8,128)} %init_ref.1, f32[32,256]{1,0:T(8,128)} %depth_ref.1, f32[32,256]{1,0:T(8,128)} %cor_ref.1, f32[32,256]{1,0:T(8,128)} %area_ref.1, f32[2,32,256]{2,1,0:T(8,128)} %face_ref.1, s32[2,64]{1,0:T(2,128)} %bitcast.2, s32[2,64]{1,0:T(2,128)} %bitcast.3, ...), custom_call_target="tpu_custom_call" | custom-call | flops 16777216 | bytes 4194304 | tf_op jit(solution)/shard_map/pallas_call | solution.py:327
  22.0 0.7 %shard_map.96 = (f32[16,4,128]{2,1,0:T(4,128)}, f32[3,32,256]{2,1,0:T(8,128)}) custom-call(f32[16,4,128]{2,1,0:T(4,128)S(1)} %get-tuple-element.4.sum_ref, f32[3,32,256]{2,1,0:T(8,128)S(1)} %get-tuple-element.5.last_ref), custom_call_target="tpu_custom_call" | custom-call | tf_op jit(solution)/shard_map/pallas_call | solution.py:369
